TPU v7x, 32 devices: a whole 2x2x4 slice. The times are simulated.
32 devices in a mesh: groups: 1, row: 16 (over z, y, x), col: 2 (over core).
Axes of the slice: x: 2, y: 2, z: 4, core: 2. Of those that a mesh axis runs over, the one named last changes fastest.
Arguments:
- wave_now: float32 [2, 2048, 4096], P('groups', 'row', 'col'), may hold values from -6 to 6
- wave_before: float32 [2, 2048, 4096], P('groups', 'row', 'col'), may hold values from -6 to 6
- fault_slip: float32 [2048, 4096], P(('groups', 'row'), 'col'), may hold values from 0 to 2
- region_ids: int32 [128, 256], P(('groups', 'row'), 'col'), may hold values from 0 to 7
- mode_history: bfloat16 [16, 2, 4096, 2048], P('groups', None, ('row', 'col')), may hold values from -6 to 6
- wave_kernel: bfloat16 [16, 4096, 2048], P(None, ('row', 'col')), may hold values from -1.5 to 1.5
- static_friction: float32 [8], replicated, may hold values from 0.55 to 0.75
- dynamic_friction: float32 [8], replicated, may hold values from 0.2 to 0.45
- weakening_slip: float32 [8], replicated, may hold values from 0.3 to 3
- normal_stress: float32 [8], replicated, may hold values from 2 to 5
- initial_stress: float32 [8], replicated, may hold values from -1.5 to 1.5
Outputs:
- final_wave: float32 [2, 2048, 4096], P('groups', 'row', 'col')
- final_slip: float32 [2048, 4096], P(('groups', 'row'), 'col')
- fault_traction: float32 [2048, 4096], P(('groups', 'row'), 'col')
All inputs are finite; a program needn't handle non-finite values.
Results may differ from a plain program's by a relative error of at most 0.0003.
Values sent between devices are 32-bit elements; how exact they have to be, the bound alone decides.
A program may use at most 128 MiB of HBM per device.

v0:
```python
import math

import jax
import jax.numpy as jnp
from jax import lax
from jax.sharding import PartitionSpec as P

SUBSTEPS = 2
BLOCK_CELLS = 16


damping = 0.5
courant = 0.3
highest = lax.Precision.HIGHEST


def with_halo(cells, sides, width):
    for axis, dim in sides:
        count = lax.axis_size(axis)
        head = lax.slice_in_dim(cells, 0, width, axis=dim)
        tail = lax.slice_in_dim(cells, cells.shape[dim] - width, cells.shape[dim], axis=dim)
        cells = jnp.concatenate(
            [
                lax.ppermute(tail, axis, [(i, (i + 1) % count) for i in range(count)]),
                cells,
                lax.ppermute(head, axis, [((i + 1) % count, i) for i in range(count)]),
            ],
            axis=dim,
        )
    return cells


def phase_table(first_count, second_count, modulus, sign):
    first = lax.broadcasted_iota(jnp.int32, (first_count, second_count), 0)
    second = lax.broadcasted_iota(jnp.int32, (first_count, second_count), 1)
    product = first * second % modulus
    angle = sign * 2.0 * math.pi / modulus * product.astype(jnp.float32)
    return (jnp.cos(angle), jnp.sin(angle))


def contract(form, left, right):
    return jnp.einsum(form, left, right, precision=highest, preferred_element_type=jnp.float32)


def complex_contract(form, left, right):
    real_part = contract(form, left[0], right[0]) - contract(form, left[1], right[1])
    imag_part = contract(form, left[0], right[1]) + contract(form, left[1], right[0])
    return (real_part, imag_part)


def complex_scale(pair, factor):
    return (pair[0] * factor[0] - pair[1] * factor[1], pair[0] * factor[1] + pair[1] * factor[0])


def forward_along_y(values):
    row_count, width = values.shape
    outer = 64
    inner = width // outer
    shaped = values.reshape(row_count, outer, inner)
    first_table = phase_table(outer, outer, outer, -1.0)
    sectioned = (
        contract("kn,rnm->rkm", first_table[0], shaped),
        contract("kn,rnm->rkm", first_table[1], shaped),
    )
    twiddle = phase_table(outer, inner, width, -1.0)
    sectioned = complex_scale(sectioned, (twiddle[0][None], twiddle[1][None]))
    second_table = phase_table(inner, inner, inner, -1.0)
    result = complex_contract("rkm,mq->qkr", sectioned, second_table)
    stacked = jnp.stack([result[0].reshape(width, row_count), result[1].reshape(width, row_count)])
    return stacked / math.sqrt(width)


def forward_along_x(pieces):
    blocks, span, block_rows = (pieces.shape[1], pieces.shape[2], pieces.shape[3])
    length = blocks * block_rows
    first_table = phase_table(blocks, blocks, blocks, -1.0)
    sectioned = complex_contract("ks,sji->kji", first_table, (pieces[0], pieces[1]))
    twiddle = phase_table(blocks, block_rows, length, -1.0)
    sectioned = complex_scale(sectioned, (twiddle[0][:, None, :], twiddle[1][:, None, :]))
    second_table = phase_table(block_rows, block_rows, block_rows, -1.0)
    result = complex_contract("kji,iq->jqk", sectioned, second_table)
    stacked = jnp.stack([result[0].reshape(span, length), result[1].reshape(span, length)])
    return stacked / math.sqrt(length)


def inverse_along_x(spectrum, blocks):
    span, length = (spectrum.shape[1], spectrum.shape[2])
    block_rows = length // blocks
    shaped = spectrum.reshape(2, span, block_rows, blocks)
    first_table = phase_table(block_rows, block_rows, block_rows, 1.0)
    sectioned = complex_contract("am,jmn->jan", first_table, (shaped[0], shaped[1]))
    twiddle = phase_table(block_rows, blocks, length, 1.0)
    sectioned = complex_scale(sectioned, (twiddle[0][None], twiddle[1][None]))
    second_table = phase_table(blocks, blocks, blocks, 1.0)
    result = complex_contract("jan,nb->bja", sectioned, second_table)
    stacked = jnp.stack(
        [result[0].reshape(blocks, span * block_rows), result[1].reshape(blocks, span * block_rows)]
    )
    return stacked / math.sqrt(length)


def inverse_along_y(spectrum):
    width, row_count = (spectrum.shape[1], spectrum.shape[2])
    outer = 64
    inner = width // outer
    shaped = spectrum.reshape(2, outer, inner, row_count)
    first_table = phase_table(outer, outer, outer, 1.0)
    sectioned = complex_contract("am,mnr->anr", first_table, (shaped[0], shaped[1]))
    twiddle = phase_table(outer, inner, width, 1.0)
    sectioned = complex_scale(sectioned, (twiddle[0][:, :, None], twiddle[1][:, :, None]))
    second_table = phase_table(inner, inner, inner, 1.0)
    real_part = contract("anr,nb->rba", sectioned[0], second_table[0]) - contract(
        "anr,nb->rba", sectioned[1], second_table[1]
    )
    return real_part.reshape(row_count, width) / math.sqrt(width)


def shards(
    wave_now,
    wave_before,
    fault_slip,
    region_ids,
    mode_history,
    wave_kernel,
    static_friction,
    dynamic_friction,
    weakening_slip,
    normal_stress,
    initial_stress,
):
    tile_rows, tile_cols = (wave_now.shape[1], wave_now.shape[2])
    row_count = lax.axis_size("row")
    col_count = lax.axis_size("col")
    col_index = lax.axis_index("col")
    blocks = row_count * col_count
    full_width = tile_cols * col_count
    span = full_width // blocks
    block_rows = region_ids.shape[0]
    block_cols = region_ids.shape[1]
    cell_ids = jnp.broadcast_to(
        region_ids[:, None, :, None], (block_rows, BLOCK_CELLS, block_cols, BLOCK_CELLS)
    ).reshape(tile_rows, tile_cols)
    region_mask = (
        cell_ids[None] == jnp.arange(static_friction.shape[0], dtype=jnp.int32)[:, None, None]
    )

    def lookup(table):
        return jnp.sum(jnp.where(region_mask, table[:, None, None], 0.0), axis=0)

    static_level = lookup(static_friction)
    dynamic_level = lookup(dynamic_friction)
    weakening = lookup(weakening_slip)
    normal_load = lookup(normal_stress)
    prestress = lookup(initial_stress)
    horizon = mode_history.shape[0]
    current = wave_now
    previous = wave_before
    slip = fault_slip
    traction = jnp.zeros_like(fault_slip)
    recent = []
    for substep in range(SUBSTEPS):
        slip_rate = current[0] - previous[0]
        padded = with_halo(current, (("row", 1), ("col", 2)), 1)
        whole_rows = lax.all_gather(slip_rate, "col", axis=1, tiled=True)
        columns = forward_along_y(whole_rows)
        own_part = lax.dynamic_index_in_dim(
            columns.reshape(2, row_count, col_count, -1), col_index, 2, keepdims=False
        )
        spread = lax.all_to_all(own_part, "row", split_axis=1, concat_axis=1, tiled=True)
        spectrum = forward_along_x(spread.reshape(2, row_count, span, tile_rows))
        recent.insert(0, spectrum)
        fresh = len(recent)
        wave_load = jnp.einsum(
            "hjk,hcjk->cjk",
            wave_kernel[fresh:],
            mode_history[: horizon - fresh],
            preferred_element_type=jnp.float32,
        )
        for offset in range(fresh):
            wave_load = wave_load + wave_kernel[offset].astype(jnp.float32)[None] * recent[offset]
        back_part = inverse_along_x(wave_load, row_count)
        returned = lax.all_to_all(back_part, "row", split_axis=1, concat_axis=1, tiled=True)
        joined = lax.all_gather(returned[:, :, None, :], "col", axis=2, tiled=True)
        whole_field = inverse_along_y(joined.reshape(2, full_width, tile_rows))
        far_field = lax.dynamic_slice_in_dim(whole_field, col_index * tile_cols, tile_cols, 1)
        trial_stress = prestress + far_field - damping * slip_rate
        strength = normal_load * (
            static_level - (static_level - dynamic_level) * jnp.minimum(slip / weakening, 1.0)
        )
        traction = jnp.clip(trial_stress, -strength, strength)
        slip = slip + jnp.abs(slip_rate)
        laplacian = (
            padded[:, 2:, 1:-1]
            + padded[:, :-2, 1:-1]
            + padded[:, 1:-1, 2:]
            + padded[:, 1:-1, :-2]
            - 4.0 * current
        )
        upper_cells = jnp.concatenate([current[1:], jnp.zeros_like(current[:1])], 0)
        lower_cells = jnp.concatenate([(current[0] + traction)[None], current[:-1]], 0)
        following = (
            2.0 * current
            - previous
            + courant * (laplacian + upper_cells + lower_cells - 2.0 * current)
        )
        previous = current
        current = following
    return (current, slip, traction)


def solution(mesh):
    return jax.shard_map(
        shards,
        mesh=mesh,
        in_specs=(
            P("groups", "row", "col"),
            P("groups", "row", "col"),
            P(("groups", "row"), "col"),
            P(("groups", "row"), "col"),
            P("groups", None, ("row", "col"), None),
            P(None, ("row", "col"), None),
            P(),
            P(),
            P(),
            P(),
            P(),
        ),
        out_specs=(
            P("groups", "row", "col"),
            P(("groups", "row"), "col"),
            P(("groups", "row"), "col"),
        ),
        check_vma=False,
    )
```

profile of v0, /device:TPU:31, one launch (start us, length us, event | category | flops | bytes accessed | tf_op | source)
XLA Modules:
  0.0 563.3 jit_solution(7440012928844400356)
XLA Ops:
  10.0 12.2 %all-gather.7.cloned.1.call-done = f32[128,4096]{1,0:T(8,128)} async-done(((f32[128,2048]{1,0:T(8,128)}), f32[128,4096]{1,0:T(8,128)}) %all-gather.7.cloned.1.call-update) | async-done | bytes 2097168 | tf_op jit(solution)/shard_map/all_gather | solution.py:164
  24.2 3.4 fusion.74
  27.6 4.5 fusion.24
  35.2 3.4 fusion.66
  41.7 3.2 add_bitcast_fusion.1
  47.4 3.5 stack.27
  53.4 4.0 stack.26
  57.5 4.3 fusion.34
  64.7 6.4 %all-to-all-start = ((f32[2,16,16384]{2,0,1:T(2,128)}), f32[2,16,16384]{2,0,1:T(2,128)}, u32[]{:S(2)}, u32[]{:S(2)}) async-start(f32[2,16,16384]{2,0,1:T(2,128)} %bitcast.290), calls=%async_computation | async-start | bytes 4194304 | tf_op jit(solution)/shard_map/all_to_all | solution.py:169
  73.9 11.0 %bitcast_convert_fusion = f32[128,2048,15]{1,0,2:T(8,128)} fusion(bf16[16,128,2048]{2,1,0:T(8,128)(2,1)} %param.16), kind=kLoop, calls=%fused_computation.8 | loop fusion | flops 3932160 | bytes 23592960
  84.9 13.7 %multiply_reduce_fusion = f32[128,2048,2]{1,0,2:T(8,128)} fusion(f32[128,2048,15]{1,0,2:T(8,128)} %bitcast_convert_fusion, bf16[16,2,128,2048]{3,2,1,0:T(8,128)(2,1)} %param.15), kind=kLoop, calls=%fused_computation | loop fusion | flops 23068672 | bytes 33554432
  100.8 16.6 %all-to-all-done = f32[2,16,16384]{2,0,1:T(2,128)} async-done(((f32[2,16,16384]{2,0,1:T(2,128)}), f32[2,16,16384]{2,0,1:T(2,128)}, u32[]{:S(2)}, u32[]{:S(2)}) %all-to-all-start) | async-done | bytes 2097184 | tf_op jit(solution)/shard_map/all_to_all | solution.py:169
  117.4 4.4 fusion.537
  152.2 51.9 %all_to_all.20 = f32[2,16,16384]{2,0,1:T(2,128)} all-to-all(f32[2,16,16384]{2,0,1:T(2,128)S(1)} %copy.494), channel_id=1, replica_groups=mesh['groups'=1,'row'=16,'col'=2] {'row'}, dimensions={1} | all-to-all | bytes 4194304 | tf_op jit(solution)/shard_map/all_to_all | solution.py:182
  206.9 4.0 collective-permute-start.1
  210.9 5.2 broadcast_in_dim.79
  216.1 8.1 %eq.44 = s32[128,2048]{1,0:T(8,128)S(1)} reshape(s32[8,16,128,16]{3,2,1,0:T(8,128)} %broadcast_in_dim.79) | data formatting | bytes 2097152 | tf_op jit(solution)/shard_map/eq | solution.py:144
  225.7 7.2 %select_reduce_fusion.2 = (f32[128,2048]{1,0:T(8,128)}, f32[128,2048]{1,0:T(8,128)}, f32[128,2048]{1,0:T(8,128)}, f32[128,2048]{1,0:T(8,128)}, f32[128,2048]{1,0:T(8,128)}) fusion(f32[8]{0:T(128)S(1)} %copy-done.24, s32[128,2048]{1,0:T(8,128)S(1)} %eq.44, f32[8]{0:T(128)S(1)} %copy-done.25, f32[8]{0:T(128)S(1)} %copy-done.26, f32[8]{0:T(128)S(1)} %copy-done.27, ...), kind=kLoop, calls=%fused_computation.4 | loop fusion | flops 21757952 | bytes 6291616 | tf_op jit(solution)/shard_map/reduce_sum | solution.py:148
  235.9 7.7 %fusion.530 = (f32[1,16,32768]{2,0,1:T(1,128)S(1)}, f32[1,16,32768]{2,0,1:T(1,128)S(1)}) fusion(f32[2,16,32768]{2,0,1:T(2,128)} %all-gather.11.cloned.1.call-done), kind=kLoop, calls=%fused_computation.608 | loop fusion | bytes 8388608 | tf_op jit(solution)/shard_map/slice | solution.py:108
  250.0 3.3 fusion.80
  253.3 4.2 multiply_subtract_fusion.1
  260.6 3.5 multiply_bitcast_fusion.1
  269.0 4.2 fusion.109
  273.3 4.4 fusion.17
  279.8 12.2 %all-gather.9.cloned.1.call-done = f32[128,4096]{1,0:T(8,128)} async-done(((f32[128,2048]{1,0:T(8,128)}), f32[128,4096]{1,0:T(8,128)}) %all-gather.9.cloned.1.call-update) | async-done | bytes 2097168 | tf_op jit(solution)/shard_map/all_gather | solution.py:164
  295.0 5.1 fusion.54
  300.0 4.5 fusion.22
  307.6 3.3 fusion.46
  310.9 4.5 subtract_bitcast_fusion
  321.2 3.5 stack.32
  324.7 4.2 copy.520
  328.9 3.7 stack.31
  332.6 5.0 fusion.35
  340.5 6.4 %all-to-all-start.2 = ((f32[2,16,16384]{2,0,1:T(2,128)}), f32[2,16,16384]{2,0,1:T(2,128)}, u32[]{:S(2)}, u32[]{:S(2)}) async-start(f32[2,16,16384]{2,0,1:T(2,128)} %bitcast.315), calls=%async_computation.2 | async-start | bytes 4194304 | tf_op jit(solution)/shard_map/all_to_all | solution.py:169
  349.5 10.1 %bitcast_convert_fusion.1 = f32[128,2048,14]{1,0,2:T(8,128)} fusion(bf16[16,128,2048]{2,1,0:T(8,128)(2,1)} %param.16), kind=kLoop, calls=%fused_computation.9 | loop fusion | flops 3670016 | bytes 22020096
  359.6 13.3 %multiply_reduce_fusion.1 = f32[128,2048,2]{1,0,2:T(8,128)} fusion(f32[128,2048,14]{1,0,2:T(8,128)} %bitcast_convert_fusion.1, bf16[16,2,128,2048]{3,2,1,0:T(8,128)(2,1)} %param.15), kind=kLoop, calls=%fused_computation.1 | loop fusion | flops 21495808 | bytes 31457280
  372.9 3.3 copy.596
  376.2 17.0 %all-to-all-done.2 = f32[2,16,16384]{2,0,1:T(2,128)} async-done(((f32[2,16,16384]{2,0,1:T(2,128)}), f32[2,16,16384]{2,0,1:T(2,128)}, u32[]{:S(2)}, u32[]{:S(2)}) %all-to-all-start.2) | async-done | bytes 2097184 | tf_op jit(solution)/shard_map/all_to_all | solution.py:169
  393.2 4.4 fusion.533
  445.2 51.9 %all_to_all.21 = f32[2,16,16384]{2,0,1:T(2,128)} all-to-all(f32[2,16,16384]{2,0,1:T(2,128)S(1)} %copy.554), channel_id=1, replica_groups=mesh['groups'=1,'row'=16,'col'=2] {'row'}, dimensions={1} | all-to-all | bytes 4194304 | tf_op jit(solution)/shard_map/all_to_all | solution.py:182
  499.5 4.3 collective-permute-start.5
  510.1 3.8 all-gather.13.cloned.1.call-done
  513.9 7.7 %fusion.529 = (f32[1,16,32768]{2,0,1:T(1,128)S(1)}, f32[1,16,32768]{2,0,1:T(1,128)S(1)}) fusion(f32[2,16,32768]{2,0,1:T(2,128)} %all-gather.13.cloned.1.call-done), kind=kLoop, calls=%fused_computation.607 | loop fusion | bytes 8388608 | tf_op jit(solution)/shard_map/slice | solution.py:108
  527.9 3.3 fusion.90
  531.3 4.2 multiply_subtract_fusion
  538.5 3.4 multiply_bitcast_fusion
  546.8 5.9 %fusion.108 = (f32[1,128,2048]{2,1,0:T(8,128)S(1)}, f32[128,2048]{1,0:T(8,128)}) fusion(f32[2,128,2048]{2,1,0:T(8,128)} %copy-done.1, f32[128,2048]{1,0:T(8,128)} %get-tuple-element.18, f32[128,2048]{1,0:T(8,128)} %get-tuple-element.13, f32[128,2048]{1,0:T(8,128)} %copy.644, f32[128,2048]{1,0:T(8,128)} %get-tuple-element.16, ...), kind=kLoop, calls=%fused_computation.161 | loop fusion | flops 3932160 | bytes 12582912 | tf_op jit(solution)/shard_map/broadcast_in_dim | solution.py:200
  552.7 3.8 fusion.8
  (184 shorter events, 165.4 us)
Async XLA Ops:
  7.2 15.1 %all-gather.7.cloned.1.call-start = ((), (), s32[]{:S(2)}) async-start(), calls=%async_computation.4 | async-start | bytes 3145728 | tf_op jit(solution)/shard_map/all_gather | solution.py:164
  53.4 4.0 copy-start.16
  64.7 52.7 %all-to-all-start = ((f32[2,16,16384]{2,0,1:T(2,128)}), f32[2,16,16384]{2,0,1:T(2,128)}, u32[]{:S(2)}, u32[]{:S(2)}) async-start(f32[2,16,16384]{2,0,1:T(2,128)} %bitcast.290), calls=%async_computation | async-start | bytes 4194304 | tf_op jit(solution)/shard_map/all_to_all | solution.py:169
  71.1 164.9 %all-gather.11.cloned.1.call-start = ((), (), s32[]{:S(2)}) async-start(), calls=%async_computation.6 | async-start | bytes 6291456 | tf_op jit(solution)/shard_map/all_gather | solution.py:183
  73.9 61.9 %copy-start.6 = (f32[128,2048]{0,1:T(8,128)}, f32[128,2048]{0,1:T(8,128)S(1)}, u32[]{:S(2)}) copy-start(f32[128,2048]{0,1:T(8,128)S(1)} %copy.483) | copy-start | bytes 3145732
  135.2 1.0 copy-start.8
  135.8 1.1 copy-start.10
  204.1 1.6 copy-start
  204.1 6.8 %copy-start.23 = (s32[8,128]{1,0:T(8,128)S(1)}, s32[8,128]{1,0:T(8,128)}, u32[]{:S(2)}) copy-start(s32[8,128]{1,0:T(8,128)} %param.14) | copy-start | bytes 12292
  204.1 87.9 %all-gather.9.cloned.1.call-start = ((), (), s32[]{:S(2)}) async-start(), calls=%async_computation.5 | async-start | bytes 3145728 | tf_op jit(solution)/shard_map/all_gather | solution.py:164
  205.7 27.4 %collective-permute-start = (f32[2,1,2048]{2,0,1:T(2,128)S(1)}, f32[2,1,2048]{2,0,1:T(2,128)S(1)}, u32[]{:S(2)}, u32[]{:S(2)}) collective-permute-start(f32[2,1,2048]{2,0,1:T(2,128)S(1)} %copy.641), channel_id=1, source_target_pairs={{2,0},{4,2},{6,4},{8,6},{10,8},{12,10},{14,12},{16,14},{18,16},{20... | collective-permute-start | bytes 49160 | tf_op jit(solution)/shard_map/ppermute | solution.py:26
  206.9 26.2 %collective-permute-start.1 = (f32[2,1,2048]{2,0,1:T(2,128)S(1)}, f32[2,1,2048]{2,0,1:T(2,128)S(1)}, u32[]{:S(2)}, u32[]{:S(2)}) collective-permute-start(f32[2,1,2048]{2,0,1:T(2,128)S(1)} %copy.642), channel_id=1, source_target_pairs={{0,2},{2,4},{4,6},{6,8},{8,10},{10,12},{12,14},{14,16},{16,18},{18... | collective-permute-start | bytes 49160 | tf_op jit(solution)/shard_map/ppermute | solution.py:24
  224.2 1.5 copy-start.24
  224.2 1.5 copy-start.25
  224.2 1.5 copy-start.26
  224.2 1.5 copy-start.27
  224.2 1.5 copy-start.28
  233.9 39.3 %collective-permute-start.2 = (f32[2,130,1]{2,1,0:T(8,128)}, f32[2,130,1]{2,1,0:T(8,128)S(1)}, u32[]{:S(2)}, u32[]{:S(2)}) collective-permute-start(f32[2,130,1]{2,1,0:T(8,128)} %get-tuple-element.37), channel_id=1, source_target_pairs={{1,0},{0,1},{3,2},{2,3},{5,4},{4,5},{7,6},{6,7},{9,8},{8,9},{11,10... | collective-permute-start | bytes 3128 | tf_op jit(solution)/shard_map/ppermute | solution.py:26
  235.9 37.3 %collective-permute-start.3 = (f32[2,130,1]{2,1,0:T(8,128)}, f32[2,130,1]{2,1,0:T(8,128)}, u32[]{:S(2)}, u32[]{:S(2)}) collective-permute-start(f32[2,130,1]{2,1,0:T(8,128)} %get-tuple-element.38), channel_id=1, source_target_pairs={{0,1},{1,0},{2,3},{3,2},{4,5},{5,4},{6,7},{7,6},{8,9},{9,8},{10,11... | collective-permute-start | bytes 3128 | tf_op jit(solution)/shard_map/ppermute | solution.py:24
  265.4 3.6 copy-start.4
  269.0 4.3 copy-start.17
  269.0 4.3 copy-start.19
  269.0 4.3 copy-start.20
  273.3 4.4 copy-start.12
  277.8 2.0 copy-start.1
  294.9 5.1 copy-start.5
  340.5 52.7 %all-to-all-start.2 = ((f32[2,16,16384]{2,0,1:T(2,128)}), f32[2,16,16384]{2,0,1:T(2,128)}, u32[]{:S(2)}, u32[]{:S(2)}) async-start(f32[2,16,16384]{2,0,1:T(2,128)} %bitcast.315), calls=%async_computation.2 | async-start | bytes 4194304 | tf_op jit(solution)/shard_map/all_to_all | solution.py:169
  346.9 167.0 %all-gather.13.cloned.1.call-start = ((), (), s32[]{:S(2)}) async-start(), calls=%async_computation.7 | async-start | bytes 6291456 | tf_op jit(solution)/shard_map/all_gather | solution.py:183
  408.7 2.8 copy-start.15
  410.2 1.3 copy-start.7
  410.3 1.5 copy-start.9
  410.3 1.8 copy-start.11
  410.3 2.1 copy-start.18
  419.4 2.6 copy-start.13
  419.4 3.9 copy-start.14
  498.2 8.7 %copy-start.2 = (f32[2,128,2048]{2,1,0:T(8,128)S(1)}, f32[2,128,2048]{2,1,0:T(8,128)}, u32[]{:S(2)}) copy-start(f32[2,128,2048]{2,1,0:T(8,128)} %copy-done.1) | copy-start | bytes 6291460
  498.2 8.7 %collective-permute-start.4 = (f32[2,1,2048]{2,0,1:T(2,128)S(1)}, f32[2,1,2048]{2,0,1:T(2,128)S(1)}, u32[]{:S(2)}, u32[]{:S(2)}) collective-permute-start(f32[2,1,2048]{2,0,1:T(2,128)S(1)} %copy.507), channel_id=1, source_target_pairs={{2,0},{4,2},{6,4},{8,6},{10,8},{12,10},{14,12},{16,14},{18,16},{20... | collective-permute-start | bytes 49160 | tf_op jit(solution)/shard_map/ppermute | solution.py:26
  499.5 7.5 %collective-permute-start.5 = (f32[2,1,2048]{2,0,1:T(2,128)S(1)}, f32[2,1,2048]{2,0,1:T(2,128)S(1)}, u32[]{:S(2)}, u32[]{:S(2)}) collective-permute-start(f32[2,1,2048]{2,0,1:T(2,128)S(1)} %copy.509), channel_id=1, source_target_pairs={{0,2},{2,4},{4,6},{6,8},{8,10},{10,12},{12,14},{14,16},{16,18},{18... | collective-permute-start | bytes 49160 | tf_op jit(solution)/shard_map/ppermute | solution.py:24
  507.8 44.9 %collective-permute-start.6 = (f32[2,130,1]{2,1,0:T(8,128)}, f32[2,130,1]{2,1,0:T(8,128)S(1)}, u32[]{:S(2)}, u32[]{:S(2)}) collective-permute-start(f32[2,130,1]{2,1,0:T(8,128)} %get-tuple-element.35), channel_id=1, source_target_pairs={{1,0},{0,1},{3,2},{2,3},{5,4},{4,5},{7,6},{6,7},{9,8},{8,9},{11,10... | collective-permute-start | bytes 3128 | tf_op jit(solution)/shard_map/ppermute | solution.py:26
  510.1 42.6 %collective-permute-start.7 = (f32[2,130,1]{2,1,0:T(8,128)}, f32[2,130,1]{2,1,0:T(8,128)S(1)}, u32[]{:S(2)}, u32[]{:S(2)}) collective-permute-start(f32[2,130,1]{2,1,0:T(8,128)} %get-tuple-element.36), channel_id=1, source_target_pairs={{0,1},{1,0},{2,3},{3,2},{4,5},{5,4},{6,7},{7,6},{8,9},{9,8},{10,11... | collective-permute-start | bytes 3128 | tf_op jit(solution)/shard_map/ppermute | solution.py:24
  546.7 5.9 %copy-start.3 = (f32[2,128,2048]{2,1,0:T(8,128)S(1)}, f32[2,128,2048]{2,1,0:T(8,128)}, u32[]{:S(2)}) copy-start(f32[2,128,2048]{2,1,0:T(8,128)} %copy-done.1) | copy-start | bytes 6291460
  546.7 6.0 %copy-start.21 = (f32[1,128,2048]{2,1,0:T(8,128)S(1)}, f32[1,128,2048]{2,1,0:T(8,128)}, u32[]{:S(2)}) copy-start(f32[1,128,2048]{2,1,0:T(8,128)} %get-tuple-element.47) | copy-start | bytes 3145732
  546.7 6.0 %copy-start.22 = (f32[1,128,2048]{2,1,0:T(8,128)S(1)}, f32[1,128,2048]{2,1,0:T(8,128)}, u32[]{:S(2)}) copy-start(f32[1,128,2048]{2,1,0:T(8,128)} %get-tuple-element.48) | copy-start | bytes 3145732
Sparse Core Ops, SparseCore 0:
  10.0 12.2 all-gather.6
  204.2 16.1 all-gather.10
  279.9 12.0 all-gather.8
  497.3 16.5 all-gather.12
where the time goes:
time: 575 us; the launch traced here: 563 us
  matrix products  135 us (23%)
  local copies, waits for them, and re-layouts  125 us (22%)
  blocking collectives  104 us (18%)
  other arithmetic  94.6 us (16%)
  waiting for transfers between devices  62 us (11%)
  starting transfers between devices  27.8 us (5%)
  between operations  15.1 us (3%)
    dot_general x56, matrix products, contract(): jnp.einsum(form, left, right, precision=highest, preferred_element_type=j...  135 us
    all_to_all x2, blocking collectives, shards(): lax.all_to_all(back_part, 'row', split_axis=1, concat_axis=1, tiled=True)  104 us
    unnamed x4, other arithmetic  48.1 us
    all_to_all x2, waiting for transfers between devices, shards(): lax.all_to_all(own_part, 'row', split_axis=1, concat_axis=1, tiled=True)  33.6 us
    all_gather x2, waiting for transfers between devices, shards(): whole_rows = lax.all_gather(slip_rate, 'col', axis=1, tiled=True)  24.4 us
    slice x2, local copies, waits for them, and re-layouts, inverse_along_y(): shaped[0]  15.5 us
    another operation x4, local copies, waits for them, and re-layouts, forward_along_y(): jnp.stack([result[0].reshape(width, row_count), result[1].reshape(width,...  14.7 us
    all_to_all x2, starting transfers between devices, shards(): lax.all_to_all(own_part, 'row', split_axis=1, concat_axis=1, tiled=True)  12.7 us
  transfers between devices with their start and end apart: 14, of which 5 were waited for; matrix products, arithmetic and copies ran while one was open for 29% of the time, Pallas kernels for 0%

commit v1 on v0

--- a/solution.py
+++ b/solution.py
@@ -1,17 +1,428 @@
+import functools
 import math
 
 import jax
 import jax.numpy as jnp
+import numpy as np
 from jax import lax
+from jax.experimental import pallas as pl
+from jax.experimental.pallas import tpu as pltpu
 from jax.sharding import PartitionSpec as P
 
 SUBSTEPS = 2
 BLOCK_CELLS = 16
 
-
 damping = 0.5
 courant = 0.3
-highest = lax.Precision.HIGHEST
+CHUNKS = 2
+VMEM_BYTES = 60 * 1024 * 1024
+f32 = jnp.float32
+bf16 = jnp.bfloat16
+
+
+def split_table(table):
+    table = table.astype(np.float32)
+    high = table.astype(bf16)
+    low = (table - high.astype(np.float32)).astype(bf16)
+    return high, low
+
+
+def y_table(length, lanes):
+    count = length // lanes
+    a = np.arange(count, dtype=np.int64)[:, None, None]
+    b = np.arange(lanes, dtype=np.int64)[None, :, None]
+    q = np.arange(lanes, dtype=np.int64)[None, None, :]
+    angle = 2.0 * np.pi / length * (((count * b + a) * q) % length)
+    return split_table(np.concatenate([np.cos(angle), -np.sin(angle)], 2) / math.sqrt(length))
+
+
+def x_table(length, lanes=128):
+    count = length // lanes
+    a = np.arange(count, dtype=np.int64)[:, None, None]
+    b = np.arange(lanes, dtype=np.int64)[None, :, None]
+    k = np.arange(lanes, dtype=np.int64)[None, None, :]
+    angle = 2.0 * np.pi / length * (((count * b + a) * k) % length)
+    cos, sin = np.cos(angle), np.sin(angle)
+    top = np.concatenate([cos, -sin], 2)
+    low = np.concatenate([sin, cos], 2)
+    return split_table(np.concatenate([top, low], 1) / math.sqrt(length))
+
+
+def fft_list(re, im, sign):
+    count = len(re)
+    if count == 1:
+        return re, im
+    ere, eim = fft_list(re[0::2], im[0::2], sign)
+    ore, oim = fft_list(re[1::2], im[1::2], sign)
+    half = count // 2
+    out_re, out_im = [None] * count, [None] * count
+    for k in range(half):
+        angle = sign * 2.0 * math.pi * k / count
+        c, s = math.cos(angle), math.sin(angle)
+        if k == 0:
+            tre, tim = ore[k], oim[k]
+        elif 4 * k == count:
+            tre, tim = (-oim[k], ore[k]) if sign > 0 else (oim[k], -ore[k])
+        elif 8 * k == count:
+            r = math.sqrt(0.5)
+            tre, tim = (ore[k] - sign * oim[k]) * r, (oim[k] + sign * ore[k]) * r
+        else:
+            tre, tim = ore[k] * c - oim[k] * s, ore[k] * s + oim[k] * c
+        out_re[k], out_im[k] = ere[k] + tre, eim[k] + tim
+        out_re[k + half], out_im[k + half] = ere[k] - tre, eim[k] - tim
+    return out_re, out_im
+
+
+def halves(values):
+    high = values.astype(bf16)
+    return high, (values - high.astype(f32)).astype(bf16)
+
+
+def dot_nn(values, high, low):
+    vh, vl = halves(values)
+    dot = functools.partial(jnp.dot, preferred_element_type=f32)
+    return dot(vh, high) + (dot(vl, high) + dot(vh, low))
+
+
+def dot_nt(high, low, values):
+    vh, vl = halves(values)
+
+    def dot(left, right):
+        return lax.dot_general(left, right, (((1,), (1,)), ((), ())), preferred_element_type=f32)
+
+    return dot(high, vh) + (dot(high, vl) + dot(low, vh))
+
+
+def forward_y(s_ref, th_ref, tl_ref, out_ref, turned, mid, done):
+    rows = s_ref.shape[0]
+    count, lanes = th_ref.shape[0], th_ref.shape[1]
+    for j in range(count):
+        part = s_ref[:, j * lanes : (j + 1) * lanes].T
+        turned[j * lanes : (j + 1) * lanes, :] = jnp.concatenate([part, part], 1)
+    for a in range(count):
+        part = turned[pl.ds(a, lanes, stride=count), :].T[:rows]
+        mid[a] = dot_nn(part, th_ref[a], tl_ref[a])
+
+    @pl.loop(0, CHUNKS)
+    def _(chunk):
+        @pl.loop(0, rows // CHUNKS // 8)
+        def _(i):
+            at = pl.ds(pl.multiple_of(chunk * (rows // CHUNKS) + i * 8, 8), 8)
+            re = [mid[a, at, :lanes] for a in range(count)]
+            im = [mid[a, at, lanes:] for a in range(count)]
+            re, im = fft_list(re, im, -1.0)
+            for d in range(count):
+                out_ref[d, 0, at, :] = re[d]
+                out_ref[d, 1, at, :] = im[d]
+
+        done(chunk)
+
+
+def inverse_y(w_ref, th_ref, tl_ref, out_ref, turned, mid, ready):
+    rows = w_ref.shape[2]
+    count, lanes = th_ref.shape[0], th_ref.shape[1]
+
+    @pl.loop(0, CHUNKS)
+    def _(chunk):
+        ready(chunk)
+
+        @pl.loop(0, rows // CHUNKS // 8)
+        def _(i):
+            at = pl.ds(pl.multiple_of(chunk * (rows // CHUNKS) + i * 8, 8), 8)
+            re = [w_ref[d, 0, at, :] for d in range(count)]
+            im = [w_ref[d, 1, at, :] for d in range(count)]
+            re, im = fft_list(re, im, 1.0)
+            for a in range(count):
+                mid[a, at, :lanes] = re[a]
+                mid[a, at, lanes:] = im[a]
+
+    for a in range(count):
+        part = dot_nt(th_ref[a], tl_ref[a], mid[a])
+        turned[pl.ds(a, lanes, stride=count), :] = jnp.concatenate([part, part], 1)
+    for j in range(count):
+        part = turned[j * lanes : (j + 1) * lanes, :].T
+        out_ref[:, j * lanes : (j + 1) * lanes] = part[:rows]
+
+
+def middle(first, field, th_ref, tl_ref, hist_ref, k0_ref, k1_ref, s_ref, mid):
+    lanes = field.shape[2]
+    count = th_ref.shape[0]
+    for a in range(count):
+        at = pl.ds(a, 128, stride=count)
+        part = jnp.concatenate([field[0, at, :].T, field[1, at, :].T], 1)
+        mid[a] = dot_nn(part, th_ref[a], tl_ref[a])
+
+    @pl.loop(0, lanes // 16)
+    def _(i):
+        for j in range(2):
+            at = pl.ds(pl.multiple_of(i * 16 + 8 * j, 8), 8)
+            both = pl.ds(pl.multiple_of(i * 16, 16), 16)
+            re = [mid[a, at, :128] for a in range(count)]
+            im = [mid[a, at, 128:] for a in range(count)]
+            re, im = fft_list(re, im, -1.0)
+            for k in range(count):
+                cols = slice(k * 128, (k + 1) * 128)
+                weight = k0_ref[both, cols].astype(f32)[8 * j : 8 * j + 8]
+                if first:
+                    s_ref[0, at, cols] = re[k]
+                    s_ref[1, at, cols] = im[k]
+                re[k] = weight * re[k] + hist_ref[0, at, cols]
+                im[k] = weight * im[k] + hist_ref[1, at, cols]
+                if not first:
+                    weight = k1_ref[both, cols].astype(f32)[8 * j : 8 * j + 8]
+                    re[k] = re[k] + weight * s_ref[0, at, cols]
+                    im[k] = im[k] + weight * s_ref[1, at, cols]
+            re, im = fft_list(re, im, 1.0)
+            for a in range(count):
+                mid[a, at, :128] = re[a]
+                mid[a, at, 128:] = im[a]
+
+    for a in range(count):
+        at = pl.ds(a, 128, stride=count)
+        part = dot_nt(th_ref[a], tl_ref[a], mid[a])
+        field[0, at, :] = part[:128]
+        field[1, at, :] = part[128:]
+
+
+def field_kernel(first, *refs):
+    rate_ref, yh, yl, xh, xl, kernel_ref = refs[:6]
+    if first:
+        modes_ref, far_ref, hist1, s_ref = refs[6:10]
+        hist, k0, k1 = refs[10:13]
+        rest = refs[13:]
+    else:
+        hist_in, s_in, far_ref = refs[6:9]
+        hist, s_ref, k0, k1 = refs[9:13]
+        rest = refs[13:]
+    (strip, columns, field, returned, tile, turned, mid_y, mid_x,
+     local_sem, pair_sem, send_sem, out_sem, in_sem) = rest
+    devices, _, rows, lanes = columns.shape
+    col_count = lax.axis_size("col")
+    row_at, col_at = lax.axis_index("row"), lax.axis_index("col")
+    me = row_at * col_count + col_at
+    width = rate_ref.shape[1]
+
+    def place(p):
+        return {"row": p // col_count, "col": p % col_count}
+
+    loads = [pltpu.make_async_copy(kernel_ref.at[0], k0, local_sem.at[0])]
+    if not first:
+        loads += [
+            pltpu.make_async_copy(kernel_ref.at[1], k1, local_sem.at[1]),
+            pltpu.make_async_copy(hist_in, hist, local_sem.at[2]),
+            pltpu.make_async_copy(s_in, s_ref, local_sem.at[3]),
+        ]
+    for load in loads:
+        load.start()
+
+    barrier = pltpu.get_barrier_semaphore()
+
+    @pl.loop(1, devices)
+    def _(k):
+        pl.semaphore_signal(barrier, 1, device_id=place((me + k) % devices))
+
+    pl.semaphore_wait(barrier, devices - 1)
+
+    other = 1 - col_at
+    own_rows = pl.ds(pl.multiple_of(col_at * rows, rows), rows)
+    pair_rows = pl.ds(pl.multiple_of(other * rows, rows), rows)
+    own_cols = pl.ds(pl.multiple_of(col_at * width, width), width)
+    pair_cols = pl.ds(pl.multiple_of(other * width, width), width)
+    swap = pltpu.make_async_remote_copy(
+        src_ref=rate_ref.at[pair_rows], dst_ref=strip.at[:, own_cols],
+        send_sem=pair_sem.at[0], recv_sem=pair_sem.at[1], device_id=place(me + other - col_at),
+    )
+    swap.start()
+    strip[:, own_cols] = rate_ref[own_rows, :]
+    swap.wait()
+
+    part_rows = rows // CHUNKS
+
+    def forward_copy(chunk, p, source):
+        at = pl.ds(pl.multiple_of(chunk * part_rows, part_rows), part_rows)
+        to = pl.ds(pl.multiple_of(me * rows + chunk * part_rows, part_rows), part_rows)
+        return pltpu.make_async_remote_copy(
+            src_ref=columns.at[p, :, at, :], dst_ref=field.at[:, to, :],
+            send_sem=send_sem.at[chunk, p], recv_sem=out_sem.at[chunk, source], device_id=place(p),
+        )
+
+    def backward_copy(chunk, p, source):
+        at = pl.ds(pl.multiple_of(p * rows + chunk * part_rows, part_rows), part_rows)
+        to = pl.ds(pl.multiple_of(chunk * part_rows, part_rows), part_rows)
+        return pltpu.make_async_remote_copy(
+            src_ref=field.at[:, at, :], dst_ref=returned.at[me, :, to, :],
+            send_sem=send_sem.at[chunk, p], recv_sem=in_sem.at[chunk, source], device_id=place(p),
+        )
+
+    def send_columns(chunk):
+        @pl.loop(1, devices)
+        def _(k):
+            forward_copy(chunk, (me + k) % devices, me).start()
+
+    forward_y(strip, yh, yl, columns, turned, mid_y, send_columns)
+    own = pl.ds(pl.multiple_of(me * rows, rows), rows)
+    field[:, own, :] = columns[me]
+
+    if first:
+        history = functools.partial(history_body, hist, hist1)
+        horizon, span, length = kernel_ref.shape
+        pltpu.emit_pipeline(
+            history,
+            grid=(span // 16,),
+            in_specs=[
+                pl.BlockSpec((horizon, 16, length), lambda i: (0, i, 0)),
+                pl.BlockSpec((horizon, 2, 16, length), lambda i: (0, 0, i, 0)),
+            ],
+        )(kernel_ref, modes_ref)
+
+    for load in loads:
+        load.wait()
+    for chunk in range(CHUNKS):
+        @pl.loop(1, devices)
+        def _(k):
+            p = (me + k) % devices
+            forward_copy(chunk, p, p).wait_recv()
+
+    for chunk in range(CHUNKS):
+        @pl.loop(1, devices)
+        def _(k):
+            forward_copy(chunk, (me + k) % devices, me).wait_send()
+
+    middle(first, field, xh, xl, hist, k0, k1, s_ref, mid_x)
+
+    for chunk in range(CHUNKS):
+        @pl.loop(1, devices)
+        def _(k):
+            backward_copy(chunk, (me + k) % devices, me).start()
+
+    returned[me] = field[:, own, :]
+
+    def receive(chunk):
+        @pl.loop(1, devices)
+        def _(k):
+            p = (me + k) % devices
+            backward_copy(chunk, p, p).wait_recv()
+
+    inverse_y(returned, yh, yl, strip, turned, mid_y, receive)
+    swap = pltpu.make_async_remote_copy(
+        src_ref=strip.at[:, pair_cols], dst_ref=tile.at[own_rows],
+        send_sem=pair_sem.at[2], recv_sem=pair_sem.at[3], device_id=place(me + other - col_at),
+    )
+    swap.start()
+    far_ref[own_rows, :] = strip[:, own_cols]
+    for chunk in range(CHUNKS):
+        @pl.loop(1, devices)
+        def _(k):
+            backward_copy(chunk, (me + k) % devices, me).wait_send()
+
+    swap.wait()
+    far_ref[pair_rows, :] = tile[pair_rows, :]
+
+
+def history_body(h0_ref, h1_ref, k_ref, m_ref):
+    horizon, rows, length = k_ref.shape
+    wide = 256
+    at = pl.ds(pl.multiple_of(pl.program_id(0) * rows, rows), rows)
+
+    @pl.loop(0, length // wide)
+    def _(i):
+        cols = pl.ds(pl.multiple_of(i * wide, wide), wide)
+        acc = [[None, None], [None, None]]
+        for h in range(horizon - 1):
+            modes = [m_ref[h, c, :, cols].astype(f32) for c in range(2)]
+            for step in range(2):
+                if h + 1 + step < horizon:
+                    weight = k_ref[h + 1 + step, :, cols].astype(f32)
+                    for c in range(2):
+                        term = weight * modes[c]
+                        acc[step][c] = term if acc[step][c] is None else acc[step][c] + term
+        for c in range(2):
+            h0_ref[c, at, cols] = acc[0][c]
+            h1_ref[c, at, cols] = acc[1][c]
+
+
+def friction_kernel(far_ref, rate_ref, slip_ref, base_ref, now_ref, level_ref, trac_ref, slip_out, next_ref, rate_out):
+    i = pl.program_id(0)
+
+    def row(p):
+        return level_ref[p, pl.ds(i, 1), :]
+
+    static, dynamic, weakening, normal, initial = [row(p) for p in range(5)]
+    rate = rate_ref[...]
+    slip = slip_ref[...]
+    strength = normal * (static - (static - dynamic) * jnp.minimum(slip / weakening, 1.0))
+    trial = initial + far_ref[...] - damping * rate
+    traction = jnp.minimum(jnp.maximum(trial, -strength), strength)
+    trac_ref[...] = traction
+    slip_out[...] = slip + jnp.abs(rate)
+    following = base_ref[...] + courant * traction
+    next_ref[...] = following
+    rate_out[...] = following - now_ref[...]
+
+
+def params(**more):
+    return pltpu.CompilerParams(vmem_limit_bytes=VMEM_BYTES, **more)
+
+
+def shape(*dims):
+    return jax.ShapeDtypeStruct(dims, f32)
+
+
+def field_call(first, rate, tables, kernel, *more):
+    tile_rows, tile_cols = rate.shape
+    _, span, length = kernel.shape
+    col_count = lax.axis_size("col")
+    devices = lax.axis_size("row") * col_count
+    rows, width = tile_rows // col_count, tile_cols * col_count
+    vmem, anywhere = pl.BlockSpec(memory_space=pltpu.VMEM), pl.BlockSpec(memory_space=pl.ANY)
+    spectrum = (2, span, length)
+    weights = [pltpu.VMEM((span, length), bf16)] * 2
+    dma = pltpu.SemaphoreType.DMA
+    common = [
+        pltpu.VMEM((rows, width), f32),
+        pltpu.VMEM((devices, 2, rows, span), f32),
+        pltpu.VMEM((2, length, span), f32),
+        pltpu.VMEM((devices, 2, rows, span), f32),
+        pltpu.VMEM((tile_rows, tile_cols), f32),
+        pltpu.VMEM((width, 2 * rows), f32),
+        pltpu.VMEM((devices, rows, 2 * span), f32),
+        pltpu.VMEM((length // 128, span, 256), f32),
+        dma((4,)), dma((4,)), dma((CHUNKS, devices)), dma((CHUNKS, devices)), dma((CHUNKS, devices)),
+    ]
+    if first:
+        scratch = [pltpu.VMEM(spectrum, f32)] + weights
+        out = (shape(tile_rows, tile_cols), shape(*spectrum), shape(*spectrum))
+        out_specs = (vmem,) * 3
+    else:
+        scratch = [pltpu.VMEM(spectrum, f32)] * 2 + weights
+        out, out_specs = shape(tile_rows, tile_cols), vmem
+    return pl.pallas_call(
+        functools.partial(field_kernel, first),
+        out_shape=out,
+        in_specs=[vmem] * 5 + [anywhere] * (1 + len(more)),
+        out_specs=out_specs,
+        scratch_shapes=scratch + common,
+        compiler_params=params(collective_id=0 if first else 1, has_side_effects=True),
+    )(rate, *tables, kernel, *more)
+
+
+def friction_step(far, rate, slip, base, now, levels):
+    rows, cols = far.shape
+    tile = pl.BlockSpec((BLOCK_CELLS, cols), lambda i: (i, 0))
+    return pl.pallas_call(
+        friction_kernel,
+        grid=(rows // BLOCK_CELLS,),
+        out_shape=(shape(rows, cols),) * 4,
+        in_specs=[tile] * 5 + [pl.BlockSpec(levels.shape, lambda i: (0, 0, 0))],
+        out_specs=(tile,) * 4,
+        compiler_params=params(),
+    )(far, rate, slip, base, now, levels)
+
+
+def block_levels(region_ids, tables):
+    mask = region_ids[None] == jnp.arange(tables[0].shape[0], dtype=jnp.int32)[:, None, None]
+    picked = jnp.stack([jnp.sum(jnp.where(mask, t[:, None, None], 0.0), axis=0) for t in tables])
+    return jnp.repeat(picked, BLOCK_CELLS, axis=2)
 
 
 def with_halo(cells, sides, width):
@@ -30,6 +441,68 @@
     return cells
 
 
+def wave_base(current, previous):
+    padded = with_halo(current, (("row", 1), ("col", 2)), 1)
+    laplacian = (
+        padded[:, 2:, 1:-1]
+        + padded[:, :-2, 1:-1]
+        + padded[:, 1:-1, 2:]
+        + padded[:, 1:-1, :-2]
+        - 4.0 * current
+    )
+    upper = jnp.concatenate([current[1:], jnp.zeros_like(current[:1])], 0)
+    lower = jnp.concatenate([current[:1], current[:-1]], 0)
+    return 2.0 * current - previous + courant * (laplacian + upper + lower - 2.0 * current)
+
+
+def shards(
+    wave_now,
+    wave_before,
+    fault_slip,
+    region_ids,
+    mode_history,
+    wave_kernel,
+    static_friction,
+    dynamic_friction,
+    weakening_slip,
+    normal_stress,
+    initial_stress,
+):
+    tile_rows, tile_cols = (wave_now.shape[1], wave_now.shape[2])
+    col_count = lax.axis_size("col")
+    devices = lax.axis_size("row") * col_count
+    width = tile_cols * col_count
+    span = wave_kernel.shape[1]
+    length = wave_kernel.shape[2]
+    rows = tile_rows // col_count
+    if span != 128 or rows % (8 * CHUNKS) or col_count != 2 or length % 128:
+        return general_shards(
+            wave_now, wave_before, fault_slip, region_ids, mode_history, wave_kernel,
+            static_friction, dynamic_friction, weakening_slip, normal_stress, initial_stress,
+        )
+    yh, yl = [jnp.asarray(t) for t in y_table(width, span)]
+    xh, xl = [jnp.asarray(t) for t in x_table(length)]
+    tables = (yh, yl, xh, xl)
+    levels = block_levels(
+        region_ids, (static_friction, dynamic_friction, weakening_slip, normal_stress, initial_stress)
+    )
+    current, previous, slip = wave_now, wave_before, fault_slip
+    rate = current[0] - previous[0]
+    for substep in range(SUBSTEPS):
+        base = wave_base(current, previous)
+        if substep == 0:
+            far, hist, spectrum = field_call(True, rate, tables, wave_kernel, mode_history)
+        else:
+            far = field_call(False, rate, tables, wave_kernel, hist, spectrum)
+        traction, slip, top, rate = friction_step(far, rate, slip, base[0], current[0], levels)
+        previous = current
+        current = jnp.stack([top, base[1]])
+    return (current, slip, traction)
+
+
+highest = lax.Precision.HIGHEST
+
+
 def phase_table(first_count, second_count, modulus, sign):
     first = lax.broadcasted_iota(jnp.int32, (first_count, second_count), 0)
     second = lax.broadcasted_iota(jnp.int32, (first_count, second_count), 1)
@@ -115,7 +588,7 @@
     return real_part.reshape(row_count, width) / math.sqrt(width)
 
 
-def shards(
+def general_shards(
     wave_now,
     wave_before,
     fault_slip,

time: 575 us -> 304 us (0.53); the launches traced: 563 us -> 303 us
  Pallas kernels: 0 us -> 262 us
  matrix products: 135 us -> 0 us
  local copies, waits for them, and re-layouts: 125 us -> 12.6 us
  blocking collectives: 104 us -> 0 us
  other arithmetic: 94.6 us -> 15.8 us
  waiting for transfers between devices: 62 us -> 5.02 us
  starting transfers between devices: 27.8 us -> 6.55 us
  between operations: 15.1 us -> 0.87 us
    pallas_call x0 -> x4, Pallas kernels: none -> 262 us  [the longest x2 248 us: field_call(): pl.pallas_call(functools.partial(field_kernel, first), out_shape=out, in_...]
    dot_general x56 -> x0, matrix products: 135 us -> none  [contract(): jnp.einsum(form, left, right, precision=highest, preferred_element_type=j...]
    all_to_all x2 -> x0, blocking collectives: 104 us -> none  [shards(): lax.all_to_all(back_part, 'row', split_axis=1, concat_axis=1, tiled=True)]
    unnamed x4 -> x0, other arithmetic: 48.1 us -> none
    all_to_all x2 -> x0, waiting for transfers between devices: 33.6 us -> none  [shards(): lax.all_to_all(own_part, 'row', split_axis=1, concat_axis=1, tiled=True)]
    slice x9 -> x1, local copies, waits for them, and re-layouts: 30.4 us -> 1.2 us  [shards(): current = jnp.stack([top, base[1]])]
    all_gather x4 -> x0, waiting for transfers between devices: 28.2 us -> none  [the longest x2 24.4 us: shards(): whole_rows = lax.all_gather(slip_rate, 'col', axis=1, tiled=True)]
    another operation x8 -> x1, local copies, waits for them, and re-layouts: 19.9 us -> 0.01 us  [block_levels(): jnp.stack([jnp.sum(jnp.where(mask, t[:, None, None], 0.0), axis=0) for t...]
  transfers between devices with their start and end apart: 14 -> 8, of which waited for: 5 -> 3; matrix products, arithmetic and copies ran while one was open for 29% -> 3% of each run, Pallas kernels for 0% -> 82%
where the time goes in v1:
time: 304 us; the launch traced here: 303 us
  Pallas kernels  262 us (86%)
  other arithmetic  15.8 us (5%)
  local copies, waits for them, and re-layouts  12.6 us (4%)
  starting transfers between devices  6.55 us (2%)
  waiting for transfers between devices  5.02 us (2%)
    pallas_call x2, Pallas kernels, field_call(): pl.pallas_call(functools.partial(field_kernel, first), out_shape=out, in_...  248 us
    pallas_call x2, Pallas kernels, friction_step(): pl.pallas_call(friction_kernel, grid=(rows // BLOCK_CELLS,), out_shape=(s...  14.3 us
    add x2, other arithmetic, wave_base(): 2.0 * current - previous  10.6 us
    ppermute x4, starting transfers between devices, with_halo(): lax.ppermute(head, axis, [((i + 1) % count, i) for i in range(count)])  6.28 us
  transfers between devices with their start and end apart: 8, of which 3 were waited for; matrix products, arithmetic and copies ran while one was open for 3% of the time, Pallas kernels for 82%

profile of v1, /device:TPU:31, one launch (start us, length us, event | category | flops | bytes accessed | tf_op | source)
XLA Modules:
  0.0 303.1 jit_solution(6752848968168956687)
XLA Ops:
  0.6 1.0 fusion.21
  1.6 0.1 collective-permute-start.1
  1.7 0.0 copy-start.3
  1.7 0.0 copy-start.4
  1.7 0.0 copy-start.5
  1.7 0.0 copy-start.6
  1.7 0.0 copy-start.7
  1.8 0.0 copy-start.8
  1.8 0.0 copy-start
  1.8 0.0 copy-start.2
  1.8 1.5 collective-permute-start
  3.3 3.2 %slice_bitcast_fusion.2 = (f32[128,2048]{1,0:T(8,128)}, f32[1,128,2048]{2,1,0:T(8,128)S(1)}, f32[1,128,2048]{2,1,0:T(8,128)}) fusion(f32[2,128,2048]{2,1,0:T(8,128)} %param.15), kind=kLoop, calls=%fused_computation.68 | loop fusion | bytes 5242880 | tf_op jit(solution)/shard_map/squeeze | solution.py:490
  6.5 0.0 copy-done.3
  6.5 0.0 copy-done.4
  6.5 0.0 copy-done.5
  6.5 0.0 copy-done.6
  6.5 0.0 copy-done.7
  6.5 0.0 copy-done.8
  6.5 0.1 select_reduce_fusion
  6.7 1.1 bitcast_subtract_fusion.refs_0_.rate_ref
  7.8 0.0 collective-permute-done.1
  7.8 0.2 collective-permute-done
  8.0 0.1 pad_maximum_fusion.29
  8.1 1.9 collective-permute-start.2
  10.0 0.1 collective-permute-start.3
  10.1 1.9 broadcast_in_dim.52
  12.0 4.0 %reshape.15.level_ref = f32[5,8,2048]{2,1,0:T(8,128)} reshape(f32[5,8,128,16]{3,2,1,0:T(8,128)} %broadcast_in_dim.52) | data formatting | bytes 655360 | tf_op jit(solution)/shard_map/reshape | solution.py:425
  16.0 124.4 %shard_map.166 = (f32[128,2048]{1,0:T(8,128)}, f32[2,128,2048]{2,1,0:T(8,128)}, f32[2,128,2048]{2,1,0:T(8,128)}) custom-call(f32[128,2048]{1,0:T(8,128)} %bitcast_subtract_fusion.refs_0_.rate_ref, bf16[32,128,256]{2,1,0:T(8,128)(2,1)} %constant.7.clone.refs_1_, bf16[32,128,256]{2,1,0:T(8,128)(2,1)} %constant.18.clone.refs_2_, ...), custom_call_target="tpu_custom_call" | custom-call | tf_op jit(solution)/shard_map/pallas_call | solution.py:399
  140.4 0.0 collective-permute-done.2
  140.4 0.0 collective-permute-done.3
  140.4 5.2 %fusion.15 = f32[2,128,2048]{2,1,0:T(8,128)S(1)} fusion(f32[2,130,1]{2,1,0:T(8,128)} %collective-permute-done.3, f32[2,1,2048]{2,1,0:T(1,128)S(1)} %collective-permute-done, f32[2,128,2048]{2,1,0:T(8,128)S(1)} %copy-done, f32[2,1,2048]{2,1,0:T(1,128)S(1)} %collective-permute-done.1, f32[2,130,1]{2,1,0:T(8,128)} %collective-permute-done.2, ...), kind=kLoop, calls=%fused_computation.34 | loop fusion | flops 11010048 | bytes 8423456 | tf_op jit(solution)/shard_map/add | solution.py:455
  145.6 1.2 fusion.20
  146.8 7.1 %shard_map.167 = (f32[128,2048]{1,0:T(8,128)}, f32[128,2048]{1,0:T(8,128)}, f32[128,2048]{1,0:T(8,128)}, f32[128,2048]{1,0:T(8,128)}) custom-call(f32[128,2048]{1,0:T(8,128)} %get-tuple-element.12.far_ref, f32[128,2048]{1,0:T(8,128)} %bitcast_subtract_fusion.refs_0_.rate_ref, f32[128,2048]{1,0:T(8,128)} %slip_ref.1, f32[128,2048]{1,0:T(8,128)} %get-tuple-element.35.base_ref, ...), custom_call_target="tpu_custom_call" | custom-call | tf_op jit(solution)/shard_map/pallas_call | solution.py:412
  153.9 1.0 fusion.19
  154.9 0.1 collective-permute-start.5
  155.0 1.5 collective-permute-start.4
  156.4 1.1 collective-permute-done.5
  157.6 3.7 %collective-permute-done.4 = f32[2,1,2048]{2,1,0:T(1,128)S(1)} collective-permute-done((f32[2,1,2048]{2,1,0:T(1,128)S(1)}, f32[2,1,2048]{2,1,0:T(1,128)S(1)}, u32[]{:S(2)}, u32[]{:S(2)}) %collective-permute-start.4) | collective-permute-done | bytes 16416 | tf_op jit(solution)/shard_map/ppermute | solution.py:437
  161.2 0.1 pad_maximum_fusion.26
  161.3 1.5 collective-permute-start.6
  162.8 0.1 collective-permute-start.7
  162.9 123.6 %shard_map.168.far_ref = f32[128,2048]{1,0:T(8,128)} custom-call(f32[128,2048]{1,0:T(8,128)} %get-tuple-element.13.refs_0_.rate_ref, bf16[32,128,256]{2,1,0:T(8,128)(2,1)} %constant.7.clone.refs_1_, bf16[32,128,256]{2,1,0:T(8,128)(2,1)} %constant.18.clone.refs_2_, bf16[16,256,256]{2,1,0:T(8,128)(2,1)} %constant.19.clone.refs_3_, ...), custom_call_target="tpu_custom_call" | custom-call | tf_op jit(solution)/shard_map/pallas_call | solution.py:399
  286.5 0.0 collective-permute-done.6
  286.5 0.0 collective-permute-done.7
  286.5 5.4 %fusion.3 = f32[2,128,2048]{2,1,0:T(8,128)S(1)} fusion(f32[1,128,2048]{2,1,0:T(8,128)} %bitcast.24, f32[2,130,1]{2,1,0:T(8,128)S(1)} %collective-permute-done.7, f32[2,1,2048]{2,1,0:T(1,128)S(1)} %collective-permute-done.4, f32[2,1,2048]{2,1,0:T(1,128)S(1)} %collective-permute-done.5, f32[1,128,2048]{2,1,0:T(8,128)S(1)} %get-tuple-element.34, ...), kind=kLoop, calls=%fused_computation.9 | loop fusion | flops 13631488 | bytes 6326304 | tf_op jit(solution)/shard_map/add | solution.py:455
  291.9 1.2 slice_bitcast_fusion
  293.1 7.2 %shard_map.169 = (f32[128,2048]{1,0:T(8,128)}, f32[128,2048]{1,0:T(8,128)}, f32[128,2048]{1,0:T(8,128)}, f32[128,2048]{1,0:T(8,128)}) custom-call(f32[128,2048]{1,0:T(8,128)} %shard_map.168.far_ref, f32[128,2048]{1,0:T(8,128)} %get-tuple-element.13.refs_0_.rate_ref, f32[128,2048]{1,0:T(8,128)} %get-tuple-element.16.slip_ref, ...), custom_call_target="tpu_custom_call" | custom-call | tf_op jit(solution)/shard_map/pallas_call | solution.py:412
  300.3 2.8 pad_maximum_fusion.22
  (9 shorter events, 0.0 us)
Async XLA Ops:
  1.6 6.2 %collective-permute-start.1 = (f32[2,1,2048]{2,1,0:T(1,128)S(1)}, f32[2,1,2048]{2,1,0:T(1,128)S(1)}, u32[]{:S(2)}, u32[]{:S(2)}) collective-permute-start(f32[2,1,2048]{2,1,0:T(1,128)S(1)} %get-tuple-element.39), channel_id=1, source_target_pairs={{0,2},{2,4},{4,6},{6,8},{8,10},{10,12},{12,14},{14,16},{16,18},{18... | collective-permute-start | bytes 49160 | tf_op jit(solution)/shard_map/ppermute | solution.py:435
  1.7 4.8 %copy-start.3 = (s32[8,128]{1,0:T(8,128)S(1)}, s32[8,128]{1,0:T(8,128)}, u32[]{:S(2)}) copy-start(s32[8,128]{1,0:T(8,128)} %param.18) | copy-start | bytes 12292
  1.7 4.8 %copy-start.4 = (f32[8]{0:T(128)S(1)}, f32[8]{0:T(128)}, u32[]{:S(2)}) copy-start(f32[8]{0:T(128)} %param.25) | copy-start | bytes 100
  1.7 4.8 %copy-start.5 = (f32[8]{0:T(128)S(1)}, f32[8]{0:T(128)}, u32[]{:S(2)}) copy-start(f32[8]{0:T(128)} %param.24) | copy-start | bytes 100
  1.7 4.8 %copy-start.6 = (f32[8]{0:T(128)S(1)}, f32[8]{0:T(128)}, u32[]{:S(2)}) copy-start(f32[8]{0:T(128)} %param.23) | copy-start | bytes 100
  1.7 4.8 %copy-start.7 = (f32[8]{0:T(128)S(1)}, f32[8]{0:T(128)}, u32[]{:S(2)}) copy-start(f32[8]{0:T(128)} %param.22) | copy-start | bytes 100
  1.8 4.8 %copy-start.8 = (f32[8]{0:T(128)S(1)}, f32[8]{0:T(128)}, u32[]{:S(2)}) copy-start(f32[8]{0:T(128)} %param.21) | copy-start | bytes 100
  1.8 4.9 %copy-start = (f32[2,128,2048]{2,1,0:T(8,128)S(1)}, f32[2,128,2048]{2,1,0:T(8,128)}, u32[]{:S(2)}) copy-start(f32[2,128,2048]{2,1,0:T(8,128)} %param.15) | copy-start | bytes 6291460
  1.8 4.9 %copy-start.2 = (f32[2,128,2048]{2,1,0:T(8,128)S(1)}, f32[2,128,2048]{2,1,0:T(8,128)}, u32[]{:S(2)}) copy-start(f32[2,128,2048]{2,1,0:T(8,128)} %param.16) | copy-start | bytes 6291460
  1.8 6.2 %collective-permute-start = (f32[2,1,2048]{2,1,0:T(1,128)S(1)}, f32[2,1,2048]{2,1,0:T(1,128)S(1)}, u32[]{:S(2)}, u32[]{:S(2)}) collective-permute-start(f32[2,1,2048]{2,1,0:T(1,128)S(1)} %get-tuple-element.40), channel_id=1, source_target_pairs={{2,0},{4,2},{6,4},{8,6},{10,8},{12,10},{14,12},{16,14},{18,16},{20... | collective-permute-start | bytes 49160 | tf_op jit(solution)/shard_map/ppermute | solution.py:437
  8.1 132.3 %collective-permute-start.2 = (f32[2,130,1]{2,1,0:T(8,128)S(1)}, f32[2,130,1]{2,1,0:T(8,128)}, u32[]{:S(2)}, u32[]{:S(2)}) collective-permute-start(f32[2,130,1]{2,1,0:T(8,128)S(1)} %get-tuple-element.28), channel_id=1, source_target_pairs={{1,0},{0,1},{3,2},{2,3},{5,4},{4,5},{7,6},{6,7},{9,8},{8,9},{11,10... | collective-permute-start | bytes 3128 | tf_op jit(solution)/shard_map/ppermute | solution.py:437
  10.0 130.4 %collective-permute-start.3 = (f32[2,130,1]{2,1,0:T(8,128)S(1)}, f32[2,130,1]{2,1,0:T(8,128)}, u32[]{:S(2)}, u32[]{:S(2)}) collective-permute-start(f32[2,130,1]{2,1,0:T(8,128)S(1)} %get-tuple-element.29), channel_id=1, source_target_pairs={{0,1},{1,0},{2,3},{3,2},{4,5},{5,4},{6,7},{7,6},{8,9},{9,8},{10,11... | collective-permute-start | bytes 3128 | tf_op jit(solution)/shard_map/ppermute | solution.py:435
  153.9 7.3 %copy-start.1 = (f32[128,2048]{1,0:T(8,128)S(1)}, f32[128,2048]{1,0:T(8,128)}, u32[]{:S(2)}) copy-start(f32[128,2048]{1,0:T(8,128)} %get-tuple-element.17.now_ref) | copy-start | bytes 3145732
  154.9 2.6 collective-permute-start.5
  155.0 6.2 %collective-permute-start.4 = (f32[2,1,2048]{2,1,0:T(1,128)S(1)}, f32[2,1,2048]{2,1,0:T(1,128)S(1)}, u32[]{:S(2)}, u32[]{:S(2)}) collective-permute-start(f32[2,1,2048]{2,1,0:T(1,128)S(1)} %get-tuple-element.33), channel_id=1, source_target_pairs={{2,0},{4,2},{6,4},{8,6},{10,8},{12,10},{14,12},{16,14},{18,16},{20... | collective-permute-start | bytes 49160 | tf_op jit(solution)/shard_map/ppermute | solution.py:437
  161.3 125.1 %collective-permute-start.6 = (f32[2,130,1]{2,1,0:T(8,128)S(1)}, f32[2,130,1]{2,1,0:T(8,128)S(1)}, u32[]{:S(2)}, u32[]{:S(2)}) collective-permute-start(f32[2,130,1]{2,1,0:T(8,128)S(1)} %get-tuple-element.26), channel_id=1, source_target_pairs={{1,0},{0,1},{3,2},{2,3},{5,4},{4,5},{7,6},{6,7},{9,8},{8,9},{11,10... | collective-permute-start | bytes 3128 | tf_op jit(solution)/shard_map/ppermute | solution.py:437
  162.8 123.7 %collective-permute-start.7 = (f32[2,130,1]{2,1,0:T(8,128)S(1)}, f32[2,130,1]{2,1,0:T(8,128)S(1)}, u32[]{:S(2)}, u32[]{:S(2)}) collective-permute-start(f32[2,130,1]{2,1,0:T(8,128)S(1)} %get-tuple-element.27), channel_id=1, source_target_pairs={{0,1},{1,0},{2,3},{3,2},{4,5},{5,4},{6,7},{7,6},{8,9},{9,8},{10,11... | collective-permute-start | bytes 3128 | tf_op jit(solution)/shard_map/ppermute | solution.py:435
